TPU v7x, 128 devices: a whole 4x4x4 slice. The times are simulated.
128 devices in a mesh: depth: 8 (over z, core), row: 16 (over y, x).
Axes of the slice: x: 4, y: 4, z: 4, core: 2. Of those that a mesh axis runs over, the one named last changes fastest.
Arguments:
- volume: float32 [384, 1024, 2048], P('depth', 'row'), may hold values from -6 to 6
- transfer: float32 [8], replicated, may hold values from 0.3 to 1.2
Outputs:
- image: float32 [4, 1024, 2048], P(None, 'row', 'depth')
All inputs are finite; a program needn't handle non-finite values.
Results may differ from a plain program's by a relative error of at most 0.0003.
Values sent between devices are 32-bit elements; how exact they have to be, the bound alone decides.
A program may use at most 192 MiB of HBM per device.

v0:
```python
import jax
import jax.numpy as jnp
from jax import lax
from jax.sharding import PartitionSpec as P


def with_halo(cells, sides, width):
    for axis, dim in sides:
        count = lax.axis_size(axis)
        ends = count - 1
        head = lax.slice_in_dim(cells, 0, width, axis=dim)
        tail = lax.slice_in_dim(cells, cells.shape[dim] - width, cells.shape[dim], axis=dim)
        cells = jnp.concatenate(
            [
                lax.ppermute(tail, axis, [(i, (i + 1) % count) for i in range(ends)]),
                cells,
                lax.ppermute(head, axis, [((i + 1) % count, i) for i in range(ends)]),
            ],
            axis=dim,
        )
    return cells


def slope_cols(center):
    zero_col = jnp.zeros_like(center[..., :1])
    right = jnp.concatenate([center[..., 1:], zero_col], -1)
    left = jnp.concatenate([zero_col, center[..., :-1]], -1)
    return 0.5 * (right - left)


def emit(framed, transfer, slices):
    center = framed[1:-1, 1:-1, :]
    slope_depth = 0.5 * (framed[2:, 1:-1, :] - framed[:-2, 1:-1, :])
    slope_row = 0.5 * (framed[1:-1, 2:, :] - framed[1:-1, :-2, :])
    slope_col = slope_cols(center)
    inverse = lax.rsqrt(
        slope_depth * slope_depth + slope_row * slope_row + slope_col * slope_col + 1.0
    )
    lambert = jnp.abs((slope_depth + 2.0 * slope_row + 2.0 * slope_col) * inverse) / 3.0
    ambient = 0.5 * transfer[7]
    shading = ambient + (1.0 - ambient) * lambert
    depth_term = 2.0 * transfer[6] / slices * jax.nn.softplus(center)
    opacity = -jnp.expm1(-depth_term)
    tinting = jax.nn.sigmoid(2.0 * center)
    weight = shading * opacity
    emitted = jnp.stack(
        [(transfer[channel] + transfer[3 + channel] * tinting) * weight for channel in range(3)]
    )
    return (emitted, depth_term)


def blend_parts(parts):
    depth_parts = parts[:, 3]
    before = jnp.cumsum(depth_parts, 0) - depth_parts
    color = jnp.sum(jnp.exp(-before)[:, None] * parts[:, :3], 0)
    total = jnp.sum(depth_parts, 0)
    return jnp.concatenate([color, total[None]], 0)


def on_device(volume, transfer):
    local_slices, local_rows, columns = volume.shape
    groups = lax.axis_size("depth")
    slices = local_slices * groups
    padded = with_halo(volume, (("depth", 0), ("row", 1)), 1)
    steps = local_slices // 8

    def march(carry, index):
        color, depth_acc = carry
        slab = lax.dynamic_slice_in_dim(padded, index * 8, 10, 0)
        emitted, depth_term = emit(slab, transfer, slices)
        before = jnp.cumsum(depth_term, 0) - depth_term
        passing = jnp.exp(-(depth_acc[None] + before))
        color = color + jnp.sum(passing[None] * emitted, 1)
        depth_acc = depth_acc + jnp.sum(depth_term, 0)
        return ((color, depth_acc), None)

    start_color = jnp.zeros((3, local_rows, columns), jnp.float32)
    start_depth = jnp.zeros((local_rows, columns), jnp.float32)
    (color, depth_acc), unused = lax.scan(
        march, (start_color, start_depth), jnp.arange(steps, dtype=jnp.int32)
    )
    partial_image = jnp.concatenate([color, depth_acc[None]], 0)
    final = blend_parts(
        lax.all_to_all(partial_image[None], "depth", split_axis=3, concat_axis=0, tiled=True)
    )
    return jnp.concatenate([final[:3], -jnp.expm1(-final[3:4])], 0)


def solution(mesh):
    in_specs = (P("depth", "row", None), P())
    out_specs = P(None, "row", "depth")
    return jax.shard_map(
        on_device, mesh=mesh, in_specs=in_specs, out_specs=out_specs, check_vma=False
    )
```

profile of v0, /device:TPU:1, one launch (start us, length us, event | category | flops | bytes accessed | tf_op | source)
XLA Modules:
  0.0 481.3 jit_solution(13706453914436330940)
XLA Ops:
  12.4 10.6 %constant_dynamic-update-slice_fusion.1 = f32[50,64,2048]{2,1,0:T(8,128)S(1)} fusion(f32[50,64,2048]{2,1,0:T(8,128)S(1)} %constant_dynamic-update-slice_fusion.2, f32[48,64,2048]{2,1,0:T(8,128)} %param.4), kind=kLoop, calls=%fused_computation.28 | loop fusion | bytes 50331648
  35.0 5.5 %collective-permute-done.3 = f32[50,1,2048]{2,1,0:T(1,128)} collective-permute-done((f32[50,1,2048]{2,1,0:T(1,128)S(1)}, f32[50,1,2048]{2,1,0:T(1,128)}, u32[]{:S(2)}, u32[]{:S(2)}) %collective-permute-start.3) | collective-permute-done | bytes 409632 | tf_op jit(solution)/shard_map/ppermute | solution.py:17
  40.5 20.7 %pad_maximum_fusion = f32[50,66,2048]{2,1,0:T(8,128)} fusion(f32[50,1,2048]{2,1,0:T(1,128)} %collective-permute-done.3, f32[50,64,2048]{2,1,0:T(8,128)} %copy-done.2, f32[50,1,2048]{2,1,0:T(1,128)S(1)} %collective-permute-done.2), kind=kLoop, calls=%fused_computation.17 | loop fusion | flops 13516800 | bytes 54067200 | tf_op jit(solution)/shard_map/concatenate | solution.py:13
  61.2 343.4 %while.16 = (s32[]{:T(128)}, f32[3,64,2048]{2,1,0:T(8,128)S(1)}, f32[64,2048]{1,0:T(8,128)S(1)}, f32[]{:T(128)}, s32[6]{0:T(128)S(1)}, /*index=5*/f32[50,66,2048...) while((s32[]{:T(128)}, f32[3,64,2048]{2,1,0:T(8,128)S(1)}, ...), condition=%wide.region_4.5_spmd.clone, body=%wide.region_0.4_spmd.clone.sunk | while | flops 86507528 | bytes 139449296 | solution.py:79
  62.3 8.3 %fusion.22 = (f32[8,64,2047]{2,1,0:T(8,128)}, f32[8,64,2047]{2,1,0:T(8,128)}) fusion(f32[50,66,2048]{2,1,0:T(8,128)} %get-tuple-element.322, s32[]{:T(128)S(6)} %add.257, s32[]{:T(128)S(6)} %add.258), kind=kLoop, calls=%fused_computation.31.clone.1 | loop fusion | bytes 16769032 | tf_op jit(solution)/shard_map/while/body/eval_jaxpr/slice | solution.py:26
  71.2 18.1 %multiply_bitcast_fusion.5 = (f32[1,8,64,2048]{3,2,1,0:T(8,128)}, f32[8,64,2048]{2,1,0:T(8,128)S(1)}) fusion(f32[]{:T(128)} %bitcast.41, f32[]{:T(128)} %bitcast.42, f32[50,66,2048]{2,1,0:T(8,128)} %get-tuple-element.322, s32[]{:T(128)S(6)} %add.257, s32[]{:T(128)S(6)} %add.258, f32[]{:T(128)} %get-tuple-element.320, f32[]{:T(128)} %get-tuple-element.325, ...), kind=kLoop, calls=%fused_computation.9.clone.1 | loop fusion | flops 36700160 | bytes 37744680 | tf_op jit(solution)/shard_map/while/body/eval_jaxpr/stack | solution.py:46
  89.4 10.4 %multiply_bitcast_fusion.6 = (f32[1,8,64,2048]{3,2,1,0:T(8,128)}, f32[1,8,64,2048]{3,2,1,0:T(8,128)}, f32[64,2048]{1,0:T(8,128)S(1)}) fusion(f32[8,64,2048]{2,1,0:T(8,128)S(1)} %get-tuple-element.276, f32[]{:T(128)} %bitcast.44, f32[]{:T(128)} %bitcast.45, f32[50,66,2048]{2,1,0:T(8,128)} %get-tuple-element.322, s32[]{:T(128)S(6)} %add.257, ...), kind=kLoop, calls=%fused_computation.8.clone.1 | loop fusion | flops 18743296 | bytes 17301532 | tf_op jit(solution)/shard_map/while/body/eval_jaxpr/stack | solution.py:46
  100.0 12.9 %negate_exponential_fusion.3 = f32[8,64,2048]{2,1,0:T(8,128)S(1)} fusion(f32[64,2048]{1,0:T(8,128)S(1)} %get-tuple-element.285, f32[50,66,2048]{2,1,0:T(8,128)} %get-tuple-element.322, s32[]{:T(128)S(6)} %add.257, s32[]{:T(128)S(6)} %add.258, f32[]{:T(128)} %get-tuple-element.320), kind=kOutput, calls=%fused_computation.12.clone.1 | output fusion | flops 17825792 | bytes 8913416 | tf_op jit(solution)/shard_map/while/body/eval_jaxpr/jit(cumsum)/reduce_window_sum | solution.py:71
  118.6 8.3 %fusion.22 = (f32[8,64,2047]{2,1,0:T(8,128)}, f32[8,64,2047]{2,1,0:T(8,128)}) fusion(f32[50,66,2048]{2,1,0:T(8,128)} %get-tuple-element.322, s32[]{:T(128)S(6)} %add.257, s32[]{:T(128)S(6)} %add.258), kind=kLoop, calls=%fused_computation.31.clone.1 | loop fusion | bytes 16769032 | tf_op jit(solution)/shard_map/while/body/eval_jaxpr/slice | solution.py:26
  127.5 18.2 %multiply_bitcast_fusion.5 = (f32[1,8,64,2048]{3,2,1,0:T(8,128)}, f32[8,64,2048]{2,1,0:T(8,128)S(1)}) fusion(f32[]{:T(128)} %bitcast.41, f32[]{:T(128)} %bitcast.42, f32[50,66,2048]{2,1,0:T(8,128)} %get-tuple-element.322, s32[]{:T(128)S(6)} %add.257, s32[]{:T(128)S(6)} %add.258, f32[]{:T(128)} %get-tuple-element.320, f32[]{:T(128)} %get-tuple-element.325, ...), kind=kLoop, calls=%fused_computation.9.clone.1 | loop fusion | flops 36700160 | bytes 37744680 | tf_op jit(solution)/shard_map/while/body/eval_jaxpr/stack | solution.py:46
  145.8 10.4 %multiply_bitcast_fusion.6 = (f32[1,8,64,2048]{3,2,1,0:T(8,128)}, f32[1,8,64,2048]{3,2,1,0:T(8,128)}, f32[64,2048]{1,0:T(8,128)S(1)}) fusion(f32[8,64,2048]{2,1,0:T(8,128)S(1)} %get-tuple-element.276, f32[]{:T(128)} %bitcast.44, f32[]{:T(128)} %bitcast.45, f32[50,66,2048]{2,1,0:T(8,128)} %get-tuple-element.322, s32[]{:T(128)S(6)} %add.257, ...), kind=kLoop, calls=%fused_computation.8.clone.1 | loop fusion | flops 18743296 | bytes 17301532 | tf_op jit(solution)/shard_map/while/body/eval_jaxpr/stack | solution.py:46
  156.4 14.1 %negate_exponential_fusion.3 = f32[8,64,2048]{2,1,0:T(8,128)S(1)} fusion(f32[64,2048]{1,0:T(8,128)S(1)} %get-tuple-element.285, f32[50,66,2048]{2,1,0:T(8,128)} %get-tuple-element.322, s32[]{:T(128)S(6)} %add.257, s32[]{:T(128)S(6)} %add.258, f32[]{:T(128)} %get-tuple-element.320), kind=kOutput, calls=%fused_computation.12.clone.1 | output fusion | flops 17825792 | bytes 8913416 | tf_op jit(solution)/shard_map/while/body/eval_jaxpr/jit(cumsum)/reduce_window_sum | solution.py:71
  176.1 8.3 %fusion.22 = (f32[8,64,2047]{2,1,0:T(8,128)}, f32[8,64,2047]{2,1,0:T(8,128)}) fusion(f32[50,66,2048]{2,1,0:T(8,128)} %get-tuple-element.322, s32[]{:T(128)S(6)} %add.257, s32[]{:T(128)S(6)} %add.258), kind=kLoop, calls=%fused_computation.31.clone.1 | loop fusion | bytes 16769032 | tf_op jit(solution)/shard_map/while/body/eval_jaxpr/slice | solution.py:26
  185.1 18.1 %multiply_bitcast_fusion.5 = (f32[1,8,64,2048]{3,2,1,0:T(8,128)}, f32[8,64,2048]{2,1,0:T(8,128)S(1)}) fusion(f32[]{:T(128)} %bitcast.41, f32[]{:T(128)} %bitcast.42, f32[50,66,2048]{2,1,0:T(8,128)} %get-tuple-element.322, s32[]{:T(128)S(6)} %add.257, s32[]{:T(128)S(6)} %add.258, f32[]{:T(128)} %get-tuple-element.320, f32[]{:T(128)} %get-tuple-element.325, ...), kind=kLoop, calls=%fused_computation.9.clone.1 | loop fusion | flops 36700160 | bytes 37744680 | tf_op jit(solution)/shard_map/while/body/eval_jaxpr/stack | solution.py:46
  203.2 10.4 %multiply_bitcast_fusion.6 = (f32[1,8,64,2048]{3,2,1,0:T(8,128)}, f32[1,8,64,2048]{3,2,1,0:T(8,128)}, f32[64,2048]{1,0:T(8,128)S(1)}) fusion(f32[8,64,2048]{2,1,0:T(8,128)S(1)} %get-tuple-element.276, f32[]{:T(128)} %bitcast.44, f32[]{:T(128)} %bitcast.45, f32[50,66,2048]{2,1,0:T(8,128)} %get-tuple-element.322, s32[]{:T(128)S(6)} %add.257, ...), kind=kLoop, calls=%fused_computation.8.clone.1 | loop fusion | flops 18743296 | bytes 17301532 | tf_op jit(solution)/shard_map/while/body/eval_jaxpr/stack | solution.py:46
  213.8 14.2 %negate_exponential_fusion.3 = f32[8,64,2048]{2,1,0:T(8,128)S(1)} fusion(f32[64,2048]{1,0:T(8,128)S(1)} %get-tuple-element.285, f32[50,66,2048]{2,1,0:T(8,128)} %get-tuple-element.322, s32[]{:T(128)S(6)} %add.257, s32[]{:T(128)S(6)} %add.258, f32[]{:T(128)} %get-tuple-element.320), kind=kOutput, calls=%fused_computation.12.clone.1 | output fusion | flops 17825792 | bytes 8913416 | tf_op jit(solution)/shard_map/while/body/eval_jaxpr/jit(cumsum)/reduce_window_sum | solution.py:71
  233.6 8.3 %fusion.22 = (f32[8,64,2047]{2,1,0:T(8,128)}, f32[8,64,2047]{2,1,0:T(8,128)}) fusion(f32[50,66,2048]{2,1,0:T(8,128)} %get-tuple-element.322, s32[]{:T(128)S(6)} %add.257, s32[]{:T(128)S(6)} %add.258), kind=kLoop, calls=%fused_computation.31.clone.1 | loop fusion | bytes 16769032 | tf_op jit(solution)/shard_map/while/body/eval_jaxpr/slice | solution.py:26
  242.6 17.9 %multiply_bitcast_fusion.5 = (f32[1,8,64,2048]{3,2,1,0:T(8,128)}, f32[8,64,2048]{2,1,0:T(8,128)S(1)}) fusion(f32[]{:T(128)} %bitcast.41, f32[]{:T(128)} %bitcast.42, f32[50,66,2048]{2,1,0:T(8,128)} %get-tuple-element.322, s32[]{:T(128)S(6)} %add.257, s32[]{:T(128)S(6)} %add.258, f32[]{:T(128)} %get-tuple-element.320, f32[]{:T(128)} %get-tuple-element.325, ...), kind=kLoop, calls=%fused_computation.9.clone.1 | loop fusion | flops 36700160 | bytes 37744680 | tf_op jit(solution)/shard_map/while/body/eval_jaxpr/stack | solution.py:46
  260.5 10.4 %multiply_bitcast_fusion.6 = (f32[1,8,64,2048]{3,2,1,0:T(8,128)}, f32[1,8,64,2048]{3,2,1,0:T(8,128)}, f32[64,2048]{1,0:T(8,128)S(1)}) fusion(f32[8,64,2048]{2,1,0:T(8,128)S(1)} %get-tuple-element.276, f32[]{:T(128)} %bitcast.44, f32[]{:T(128)} %bitcast.45, f32[50,66,2048]{2,1,0:T(8,128)} %get-tuple-element.322, s32[]{:T(128)S(6)} %add.257, ...), kind=kLoop, calls=%fused_computation.8.clone.1 | loop fusion | flops 18743296 | bytes 17301532 | tf_op jit(solution)/shard_map/while/body/eval_jaxpr/stack | solution.py:46
  271.1 13.8 %negate_exponential_fusion.3 = f32[8,64,2048]{2,1,0:T(8,128)S(1)} fusion(f32[64,2048]{1,0:T(8,128)S(1)} %get-tuple-element.285, f32[50,66,2048]{2,1,0:T(8,128)} %get-tuple-element.322, s32[]{:T(128)S(6)} %add.257, s32[]{:T(128)S(6)} %add.258, f32[]{:T(128)} %get-tuple-element.320), kind=kOutput, calls=%fused_computation.12.clone.1 | output fusion | flops 17825792 | bytes 8913416 | tf_op jit(solution)/shard_map/while/body/eval_jaxpr/jit(cumsum)/reduce_window_sum | solution.py:71
  290.6 8.3 %fusion.22 = (f32[8,64,2047]{2,1,0:T(8,128)}, f32[8,64,2047]{2,1,0:T(8,128)}) fusion(f32[50,66,2048]{2,1,0:T(8,128)} %get-tuple-element.322, s32[]{:T(128)S(6)} %add.257, s32[]{:T(128)S(6)} %add.258), kind=kLoop, calls=%fused_computation.31.clone.1 | loop fusion | bytes 16769032 | tf_op jit(solution)/shard_map/while/body/eval_jaxpr/slice | solution.py:26
  299.5 18.2 %multiply_bitcast_fusion.5 = (f32[1,8,64,2048]{3,2,1,0:T(8,128)}, f32[8,64,2048]{2,1,0:T(8,128)S(1)}) fusion(f32[]{:T(128)} %bitcast.41, f32[]{:T(128)} %bitcast.42, f32[50,66,2048]{2,1,0:T(8,128)} %get-tuple-element.322, s32[]{:T(128)S(6)} %add.257, s32[]{:T(128)S(6)} %add.258, f32[]{:T(128)} %get-tuple-element.320, f32[]{:T(128)} %get-tuple-element.325, ...), kind=kLoop, calls=%fused_computation.9.clone.1 | loop fusion | flops 36700160 | bytes 37744680 | tf_op jit(solution)/shard_map/while/body/eval_jaxpr/stack | solution.py:46
  317.8 10.4 %multiply_bitcast_fusion.6 = (f32[1,8,64,2048]{3,2,1,0:T(8,128)}, f32[1,8,64,2048]{3,2,1,0:T(8,128)}, f32[64,2048]{1,0:T(8,128)S(1)}) fusion(f32[8,64,2048]{2,1,0:T(8,128)S(1)} %get-tuple-element.276, f32[]{:T(128)} %bitcast.44, f32[]{:T(128)} %bitcast.45, f32[50,66,2048]{2,1,0:T(8,128)} %get-tuple-element.322, s32[]{:T(128)S(6)} %add.257, ...), kind=kLoop, calls=%fused_computation.8.clone.1 | loop fusion | flops 18743296 | bytes 17301532 | tf_op jit(solution)/shard_map/while/body/eval_jaxpr/stack | solution.py:46
  328.4 14.1 %negate_exponential_fusion.3 = f32[8,64,2048]{2,1,0:T(8,128)S(1)} fusion(f32[64,2048]{1,0:T(8,128)S(1)} %get-tuple-element.285, f32[50,66,2048]{2,1,0:T(8,128)} %get-tuple-element.322, s32[]{:T(128)S(6)} %add.257, s32[]{:T(128)S(6)} %add.258, f32[]{:T(128)} %get-tuple-element.320), kind=kOutput, calls=%fused_computation.12.clone.1 | output fusion | flops 17825792 | bytes 8913416 | tf_op jit(solution)/shard_map/while/body/eval_jaxpr/jit(cumsum)/reduce_window_sum | solution.py:71
  348.2 8.3 %fusion.22 = (f32[8,64,2047]{2,1,0:T(8,128)}, f32[8,64,2047]{2,1,0:T(8,128)}) fusion(f32[50,66,2048]{2,1,0:T(8,128)} %get-tuple-element.322, s32[]{:T(128)S(6)} %add.257, s32[]{:T(128)S(6)} %add.258), kind=kLoop, calls=%fused_computation.31.clone.1 | loop fusion | bytes 16769032 | tf_op jit(solution)/shard_map/while/body/eval_jaxpr/slice | solution.py:26
  357.1 18.4 %multiply_bitcast_fusion.5 = (f32[1,8,64,2048]{3,2,1,0:T(8,128)}, f32[8,64,2048]{2,1,0:T(8,128)S(1)}) fusion(f32[]{:T(128)} %bitcast.41, f32[]{:T(128)} %bitcast.42, f32[50,66,2048]{2,1,0:T(8,128)} %get-tuple-element.322, s32[]{:T(128)S(6)} %add.257, s32[]{:T(128)S(6)} %add.258, f32[]{:T(128)} %get-tuple-element.320, f32[]{:T(128)} %get-tuple-element.325, ...), kind=kLoop, calls=%fused_computation.9.clone.1 | loop fusion | flops 36700160 | bytes 37744680 | tf_op jit(solution)/shard_map/while/body/eval_jaxpr/stack | solution.py:46
  375.5 10.4 %multiply_bitcast_fusion.6 = (f32[1,8,64,2048]{3,2,1,0:T(8,128)}, f32[1,8,64,2048]{3,2,1,0:T(8,128)}, f32[64,2048]{1,0:T(8,128)S(1)}) fusion(f32[8,64,2048]{2,1,0:T(8,128)S(1)} %get-tuple-element.276, f32[]{:T(128)} %bitcast.44, f32[]{:T(128)} %bitcast.45, f32[50,66,2048]{2,1,0:T(8,128)} %get-tuple-element.322, s32[]{:T(128)S(6)} %add.257, ...), kind=kLoop, calls=%fused_computation.8.clone.1 | loop fusion | flops 18743296 | bytes 17301532 | tf_op jit(solution)/shard_map/while/body/eval_jaxpr/stack | solution.py:46
  386.1 13.9 %negate_exponential_fusion.3 = f32[8,64,2048]{2,1,0:T(8,128)S(1)} fusion(f32[64,2048]{1,0:T(8,128)S(1)} %get-tuple-element.285, f32[50,66,2048]{2,1,0:T(8,128)} %get-tuple-element.322, s32[]{:T(128)S(6)} %add.257, s32[]{:T(128)S(6)} %add.258, f32[]{:T(128)} %get-tuple-element.320), kind=kOutput, calls=%fused_computation.12.clone.1 | output fusion | flops 17825792 | bytes 8913416 | tf_op jit(solution)/shard_map/while/body/eval_jaxpr/jit(cumsum)/reduce_window_sum | solution.py:71
  413.3 6.8 %reshape.30 = f32[8,1,65536]{2,1,0:T(1,128)S(1)} reshape(f32[2048,1,4,64]{3,2,1,0:T(4,128)} %fusion.14) | data formatting | bytes 4194304
  420.1 36.3 %all_to_all.18 = f32[8,1,65536]{2,1,0:T(1,128)} all-to-all(f32[8,1,65536]{2,1,0:T(1,128)S(1)} %reshape.30), channel_id=1, replica_groups=mesh['depth'=8,'row'=16] {'depth'}, dimensions={0} | all-to-all | bytes 4194304 | tf_op jit(solution)/shard_map/all_to_all | solution.py:84
  456.9 7.2 %reduce.1 = f32[8,65536]{1,0:T(8,128)S(1)} reduce(f32[8,1,65536]{2,1,0:T(1,128)} %all_to_all.18, f32[]{:T(128)} %broadcast.78), dimensions={1}, to_apply=%all_to_all.13.reduce_sub_computation | reduce | bytes 4194308 | tf_op jit(solution)/shard_map/all_to_all | solution.py:84
  468.9 7.7 %negate_exponential_fusion.1 = (f32[8,1,64,256]{2,1,3,0:T(1,128)S(1)}, f32[64,256]{0,1:T(8,128)S(1)}) fusion(f32[8,4,64,256]{2,1,3,0:T(4,128)} %bitcast.48), kind=kOutput, calls=%fused_computation.21 | output fusion | flops 1294336 | bytes 2686976 | tf_op jit(solution)/shard_map/jit(cumsum)/reduce_window_sum | solution.py:54
  (82 shorter events, 77.0 us)
Async XLA Ops:
  1.3 11.0 %collective-permute-start = (f32[1,64,2048]{2,1,0:T(8,128)S(1)}, f32[1,64,2048]{2,1,0:T(8,128)S(1)}, u32[]{:S(2)}, u32[]{:S(2)}) collective-permute-start(f32[1,64,2048]{2,1,0:T(8,128)S(1)} %get-tuple-element.197), channel_id=1, source_target_pairs={{0,16},{16,32},{32,48},{48,64},{64,80},{80,96},{96,112},{1,17},{17... | collective-permute-start | bytes 1572872 | tf_op jit(solution)/shard_map/ppermute | solution.py:15
  6.2 16.8 %collective-permute-start.1 = (f32[1,64,2048]{2,1,0:T(8,128)S(1)}, f32[1,64,2048]{2,1,0:T(8,128)S(1)}, u32[]{:S(2)}, u32[]{:S(2)}) collective-permute-start(f32[1,64,2048]{2,1,0:T(8,128)S(1)} %get-tuple-element.196), channel_id=1, source_target_pairs={{16,0},{32,16},{48,32},{64,48},{80,64},{96,80},{112,96},{17,1},{33... | collective-permute-start | bytes 1572872 | tf_op jit(solution)/shard_map/ppermute | solution.py:17
  12.4 20.7 %copy-start.3 = (f32[8]{0:T(128)S(1)}, f32[8]{0:T(128)}, u32[]{:S(2)}) copy-start(f32[8]{0:T(128)} %param.5) | copy-start | bytes 100
  23.1 8.6 %copy-start.2 = (f32[50,64,2048]{2,1,0:T(8,128)}, f32[50,64,2048]{2,1,0:T(8,128)S(1)}, u32[]{:S(2)}) copy-start(f32[50,64,2048]{2,1,0:T(8,128)S(1)} %constant_dynamic-update-slice_fusion) | copy-start | bytes 78643200
  23.9 11.1 %collective-permute-start.2 = (f32[50,1,2048]{2,1,0:T(1,128)S(1)}, f32[50,1,2048]{2,1,0:T(1,128)S(1)}, u32[]{:S(2)}, u32[]{:S(2)}) collective-permute-start(f32[50,1,2048]{2,1,0:T(1,128)S(1)} %get-tuple-element.194), channel_id=1, source_target_pairs={{0,1},{1,2},{2,3},{3,4},{4,5},{5,6},{6,7},{7,8},{8,9},{9,10},{10,1... | collective-permute-start | bytes 1228808 | tf_op jit(solution)/shard_map/ppermute | solution.py:15
  31.7 8.8 %collective-permute-start.3 = (f32[50,1,2048]{2,1,0:T(1,128)S(1)}, f32[50,1,2048]{2,1,0:T(1,128)}, u32[]{:S(2)}, u32[]{:S(2)}) collective-permute-start(f32[50,1,2048]{2,1,0:T(1,128)S(1)} %get-tuple-element.195), channel_id=1, source_target_pairs={{1,0},{2,1},{3,2},{4,3},{5,4},{6,5},{7,6},{8,7},{9,8},{10,9},{11,1... | collective-permute-start | bytes 1228808 | tf_op jit(solution)/shard_map/ppermute | solution.py:17
  100.0 12.9 %copy-start = (f32[1,8,64,2048]{3,2,1,0:T(8,128)S(1)}, f32[1,8,64,2048]{3,2,1,0:T(8,128)}, u32[]{:S(2)}) copy-start(f32[1,8,64,2048]{3,2,1,0:T(8,128)} %get-tuple-element.283) | copy-start | bytes 12582916 | tf_op jit(solution)/shard_map/while
  100.0 12.9 %copy-start.1 = (f32[1,8,64,2048]{3,2,1,0:T(8,128)S(1)}, f32[1,8,64,2048]{3,2,1,0:T(8,128)}, u32[]{:S(2)}) copy-start(f32[1,8,64,2048]{3,2,1,0:T(8,128)} %get-tuple-element.282) | copy-start | bytes 12582916 | tf_op jit(solution)/shard_map/while
  156.4 14.1 %copy-start = (f32[1,8,64,2048]{3,2,1,0:T(8,128)S(1)}, f32[1,8,64,2048]{3,2,1,0:T(8,128)}, u32[]{:S(2)}) copy-start(f32[1,8,64,2048]{3,2,1,0:T(8,128)} %get-tuple-element.283) | copy-start | bytes 12582916 | tf_op jit(solution)/shard_map/while
  156.4 14.1 %copy-start.1 = (f32[1,8,64,2048]{3,2,1,0:T(8,128)S(1)}, f32[1,8,64,2048]{3,2,1,0:T(8,128)}, u32[]{:S(2)}) copy-start(f32[1,8,64,2048]{3,2,1,0:T(8,128)} %get-tuple-element.282) | copy-start | bytes 12582916 | tf_op jit(solution)/shard_map/while
  213.8 14.2 %copy-start = (f32[1,8,64,2048]{3,2,1,0:T(8,128)S(1)}, f32[1,8,64,2048]{3,2,1,0:T(8,128)}, u32[]{:S(2)}) copy-start(f32[1,8,64,2048]{3,2,1,0:T(8,128)} %get-tuple-element.283) | copy-start | bytes 12582916 | tf_op jit(solution)/shard_map/while
  213.8 14.2 %copy-start.1 = (f32[1,8,64,2048]{3,2,1,0:T(8,128)S(1)}, f32[1,8,64,2048]{3,2,1,0:T(8,128)}, u32[]{:S(2)}) copy-start(f32[1,8,64,2048]{3,2,1,0:T(8,128)} %get-tuple-element.282) | copy-start | bytes 12582916 | tf_op jit(solution)/shard_map/while
  271.1 13.8 %copy-start = (f32[1,8,64,2048]{3,2,1,0:T(8,128)S(1)}, f32[1,8,64,2048]{3,2,1,0:T(8,128)}, u32[]{:S(2)}) copy-start(f32[1,8,64,2048]{3,2,1,0:T(8,128)} %get-tuple-element.283) | copy-start | bytes 12582916 | tf_op jit(solution)/shard_map/while
  271.1 13.8 %copy-start.1 = (f32[1,8,64,2048]{3,2,1,0:T(8,128)S(1)}, f32[1,8,64,2048]{3,2,1,0:T(8,128)}, u32[]{:S(2)}) copy-start(f32[1,8,64,2048]{3,2,1,0:T(8,128)} %get-tuple-element.282) | copy-start | bytes 12582916 | tf_op jit(solution)/shard_map/while
  328.4 14.2 %copy-start = (f32[1,8,64,2048]{3,2,1,0:T(8,128)S(1)}, f32[1,8,64,2048]{3,2,1,0:T(8,128)}, u32[]{:S(2)}) copy-start(f32[1,8,64,2048]{3,2,1,0:T(8,128)} %get-tuple-element.283) | copy-start | bytes 12582916 | tf_op jit(solution)/shard_map/while
  328.4 14.2 %copy-start.1 = (f32[1,8,64,2048]{3,2,1,0:T(8,128)S(1)}, f32[1,8,64,2048]{3,2,1,0:T(8,128)}, u32[]{:S(2)}) copy-start(f32[1,8,64,2048]{3,2,1,0:T(8,128)} %get-tuple-element.282) | copy-start | bytes 12582916 | tf_op jit(solution)/shard_map/while
  386.1 13.9 %copy-start = (f32[1,8,64,2048]{3,2,1,0:T(8,128)S(1)}, f32[1,8,64,2048]{3,2,1,0:T(8,128)}, u32[]{:S(2)}) copy-start(f32[1,8,64,2048]{3,2,1,0:T(8,128)} %get-tuple-element.283) | copy-start | bytes 12582916 | tf_op jit(solution)/shard_map/while
  386.1 13.9 %copy-start.1 = (f32[1,8,64,2048]{3,2,1,0:T(8,128)S(1)}, f32[1,8,64,2048]{3,2,1,0:T(8,128)}, u32[]{:S(2)}) copy-start(f32[1,8,64,2048]{3,2,1,0:T(8,128)} %get-tuple-element.282) | copy-start | bytes 12582916 | tf_op jit(solution)/shard_map/while
where the time goes:
time: 484 us; the launch traced here: 481 us
  other arithmetic  327 us (68%)
  local copies, waits for them, and re-layouts  91.7 us (19%)
  blocking collectives  36.3 us (7%)
  starting transfers between devices  11.3 us (2%)
  waiting for transfers between devices  9.72 us (2%)
    another operation x12, other arithmetic, emit(): jnp.stack([(transfer[channel] + transfer[3 + channel] * tinting) * weight...  172 us
    another operation x6, other arithmetic, march(): before = jnp.cumsum(depth_term, 0) - depth_term  83 us
    slice x6, local copies, waits for them, and re-layouts, slope_cols(): right = jnp.concatenate([center[..., 1:], zero_col], -1)  49.7 us
    all_to_all x1, blocking collectives, on_device(): lax.all_to_all(partial_image[None], 'depth', split_axis=3, concat_axis=0,...  36.3 us
    unnamed x8, local copies, waits for them, and re-layouts  27 us
    reduce_sum x6, other arithmetic, march(): color = color + jnp.sum(passing[None] * emitted, 1)  23.7 us
    concatenate x1, other arithmetic, with_halo(): jnp.concatenate([lax.ppermute(tail, axis, [(i, (i + 1) % count) for i in...  20.7 us
  transfers between devices with their start and end apart: 4, of which 2 were waited for; matrix products, arithmetic and copies ran while one was open for 2% of the time, Pallas kernels for 0%

commit v1 on v0

v1 whole, which is shorter than its diff:
```python
import jax
import jax.numpy as jnp
from jax import lax
from jax.experimental import pallas as pl
from jax.experimental.pallas import tpu as pltpu
from jax.sharding import PartitionSpec as P

LOG2E = 1.4426950408889634
LN2 = 0.6931471805599453
LANES = 128
ROWS = 16
TOP = 8
MESH = pl.DeviceIdType.MESH


def block_of(depth, step):
    chip, core = depth // 2, depth % 2
    phase, half = step // 2, step % 2
    parity = core * half + (1 - core) * (1 - half)
    return 2 * ((chip + 1 + phase) % 4) + parity


def kernel(
    transfer,
    volume,
    image,
    vol,
    res,
    sib,
    parts,
    final,
    load_sem,
    halo_send,
    halo_recv,
    sib_send,
    sib_recv,
    part_send,
    part_recv,
    out_sem,
):
    depth, row = lax.axis_index("depth"), lax.axis_index("row")
    depths, rows = lax.axis_size("depth"), lax.axis_size("row")
    slices, height, _ = volume.shape
    chip, core = depth // 2, depth % 2
    sibling = depth + 1 - 2 * core
    first = 4 * ((chip + 1) % 4)

    def load(position):
        tile = (first + position) % 16
        return pltpu.make_async_copy(
            volume.at[:, :, pl.ds(pl.multiple_of(tile * LANES, LANES), LANES)],
            vol.at[tile + 1, pl.ds(1, slices), pl.ds(TOP, height), :],
            load_sem.at[tile],
        )

    lead = 2 - 2 * core
    order = [lead, lead + 1, lead + 15, lead + 2]
    second = [3 * core, 15 + 5 * core]
    for position in order + second:
        load(position).start()
    for position in range(5, 15):
        load(position).start()

    def partners(act):
        for offset in (2, 4, 6):
            act(True, {"depth": (depth + offset) % depths})
        act(depth > 0, {"depth": depth - 1})
        act(depth < depths - 1, {"depth": depth + 1})
        act(row > 0, {"row": row - 1})
        act(row < rows - 1, {"row": row + 1})

    barrier = pltpu.get_barrier_semaphore()

    def greet(there, device):
        def signal():
            pl.semaphore_signal(barrier, inc=1, device_id=device, device_id_type=MESH)

        signal() if there is True else pl.when(there)(signal)

    partners(greet)

    @pl.loop(0, slices)
    def _(z):
        vol[0, z + 1, pl.ds(TOP, height), :] = jnp.zeros((height, LANES), jnp.float32)
        vol[17, z + 1, pl.ds(TOP, height), :] = jnp.zeros((height, LANES), jnp.float32)

    def clear_slab(slab):
        @pl.loop(0, 16)
        def _(tile):
            vol[tile + 1, slab, pl.ds(TOP, height), :] = jnp.zeros((height, LANES), jnp.float32)

    def clear_row(at):
        @pl.loop(0, 16)
        def _(tile):
            @pl.loop(0, slices)
            def _(z):
                vol[tile + 1, z + 1, pl.ds(at, 1), :] = jnp.zeros((1, LANES), jnp.float32)

    pl.when(depth == 0)(lambda: clear_slab(0))
    pl.when(depth == depths - 1)(lambda: clear_slab(slices + 1))
    pl.when(row == 0)(lambda: clear_row(TOP - 1))
    pl.when(row == rows - 1)(lambda: clear_row(TOP + height))

    count = 3 + (depth > 0).astype(jnp.int32) + (depth < depths - 1).astype(jnp.int32)
    count = count + (row > 0).astype(jnp.int32) + (row < rows - 1).astype(jnp.int32)
    pl.semaphore_wait(barrier, count)

    def halo(kind, tile):
        columns = pl.ds(pl.multiple_of(tile * LANES, LANES), LANES)
        if kind < 2:
            source = volume.at[slices - 1 if kind == 0 else 0, :, columns]
            target = vol.at[tile + 1, 0 if kind == 0 else slices + 1, pl.ds(TOP, height), :]
            device = {"depth": depth + 1 if kind == 0 else depth - 1}
        else:
            source = volume.at[:, pl.ds(height - 1 if kind == 2 else 0, 1), columns]
            target = vol.at[
                tile + 1, pl.ds(1, slices), pl.ds(TOP - 1 if kind == 2 else TOP + height, 1), :
            ]
            device = {"row": row + 1 if kind == 2 else row - 1}
        return pltpu.make_async_remote_copy(
            src_ref=source,
            dst_ref=target,
            send_sem=halo_send.at[kind, tile],
            recv_sem=halo_recv.at[kind, tile],
            device_id=device,
            device_id_type=MESH,
        )

    can_send = (depth < depths - 1, depth > 0, row < rows - 1, row > 0)
    can_receive = (depth > 0, depth < depths - 1, row > 0, row < rows - 1)

    def send_halos(step):
        for kind, to in ((0, depth + 1), (1, depth - 1), (2, depth), (3, depth)):

            @pl.when(can_send[kind])
            def _(kind=kind, to=to):
                block = block_of(to, step)
                for side in range(2):
                    halo(kind, 2 * block + side).start()

    def receive_halos(kinds, block):
        for kind in kinds:

            @pl.when(can_receive[kind])
            def _(kind=kind):
                for side in range(2):
                    halo(kind, 2 * block + side).wait_recv()

    send_halos(0)
    send_halos(1)

    density = transfer[6] * (2.0 / (slices * depths))
    ambient = 0.5 * transfer[7]
    lift = 3.0 * ambient / (1.0 - ambient)
    lane = lax.broadcasted_iota(jnp.int32, (ROWS, LANES), 1)
    lowest, highest = lane == 0, lane == LANES - 1

    def march(tile, start, step):
        here = pl.ds(pl.multiple_of(TOP + start, 8), ROWS)
        above, below = pl.ds(TOP + start - 1, ROWS), pl.ds(TOP + start + 1, ROWS)

        def slab(z, carry):
            ahead, middle, logs, passing, white, tinted = carry
            behind = tuple(vol[tile + 1 + side, z + 2, here, :] for side in range(2))
            outer = (vol[tile, z + 1, here, :], vol[tile + 3, z + 1, here, :])
            lefts, rights = (outer[0], middle[0]), (middle[1], outer[1])
            out = []
            for side in range(2):
                value = middle[side]
                left = pltpu.roll(jnp.where(highest, lefts[side], value), 1, 1)
                right = pltpu.roll(jnp.where(lowest, rights[side], value), LANES - 1, 1)
                by_depth = behind[side] - ahead[side]
                by_row = vol[tile + 1 + side, z + 1, below, :] - vol[tile + 1 + side, z + 1, above, :]
                by_column = right - left
                plane = by_row + by_column
                along = by_depth + (plane + plane)
                square = (by_depth * by_depth + 4.0) + (by_row * by_row + by_column * by_column)
                lambert = jnp.abs(along) * lax.rsqrt(square)
                log = logs[side] - jnp.log2(1.0 + jnp.exp2(value * LOG2E))
                after = jnp.exp2(log * density)
                lit = (passing[side] - after) * (lambert + lift)
                out.append(
                    (log, after, white[side] + lit, tinted[side] + lit * jnp.tanh(value))
                )
            return (middle, behind) + tuple(zip(*out))

        zero = jnp.zeros((ROWS, LANES), jnp.float32)
        carry = tuple(
            tuple(vol[tile + 1 + side, z, here, :] for side in range(2)) for z in range(2)
        )
        carry = carry + ((zero,) * 2, (zero + 1.0,) * 2, (zero,) * 2, (zero,) * 2)
        _, _, logs, _, white, tinted = lax.fori_loop(0, slices, slab, carry, unroll=True)
        put = pl.ds(pl.multiple_of(start, 8), ROWS)
        for side in range(2):
            columns = pl.ds(side * LANES, LANES)
            res[step, 0, put, columns] = white[side]
            res[step, 1, put, columns] = tinted[side]
            res[step, 2, put, columns] = logs[side]

    def to_sibling(phase):
        return pltpu.make_async_remote_copy(
            src_ref=res.at[2 * phase],
            dst_ref=sib.at[phase],
            send_sem=sib_send.at[phase],
            recv_sem=sib_recv.at[phase],
            device_id={"depth": sibling},
            device_id_type=MESH,
        )

    def to_owner(phase):
        return pltpu.make_async_remote_copy(
            src_ref=res.at[2 * phase + 1],
            dst_ref=parts.at[phase],
            send_sem=part_send.at[phase],
            recv_sem=part_recv.at[phase],
            device_id={"depth": 2 * ((chip + 1 + phase) % 4) + core},
            device_id_type=MESH,
        )

    def join(phase):
        @pl.loop(0, height // ROWS)
        def _(chunk):
            at = pl.ds(pl.multiple_of(chunk * ROWS, ROWS), ROWS)
            mine = [res[2 * phase + 1, plane, at, :] for plane in range(3)]
            other = [sib[phase, plane, at, :] for plane in range(3)]
            front = [jnp.where(core == 0, a, b) for a, b in zip(mine, other)]
            back = [jnp.where(core == 0, b, a) for a, b in zip(mine, other)]
            through = jnp.exp2(front[2] * density)
            res[2 * phase + 1, 0, at, :] = front[0] + through * back[0]
            res[2 * phase + 1, 1, at, :] = front[1] + through * back[1]
            res[2 * phase + 1, 2, at, :] = front[2] + back[2]

    @pl.loop(0, 8)
    def _(step):
        block = block_of(depth, step)
        phase, half = step // 2, step % 2
        pl.when(step < 6)(lambda: send_halos(step + 2))

        @pl.when(step == 0)
        def _():
            for position in order:
                load(position).wait()

        @pl.when(step == 1)
        def _():
            for position in second:
                load(position).wait()

        @pl.when((half == 0) & (step >= 2) & (step < 6))
        def _():
            for position in range(1, 5):
                load(4 * phase + position).wait()

        @pl.when(step == 6)
        def _():
            for position in range(13, 15):
                load(position).wait()

        receive_halos((0, 1), block)

        @pl.loop(0, 2)
        def _(turn):
            pl.when(turn == 1)(lambda: receive_halos((2, 3), block))
            march(2 * block, ROWS * (1 - turn), step)
            march(2 * block, ROWS * (2 + turn), step)

        pl.when(half == 0)(lambda: to_sibling(phase).start())

        @pl.when(half == 1)
        def _():
            to_sibling(phase).wait_recv()
            join(phase)
            pl.when(phase < 3)(lambda: to_owner(phase).start())

    for phase in range(3):
        to_owner(phase).wait_recv()

    scale = (1.0 - ambient) / 3.0
    slope = [scale * 0.5 * transfer[3 + colour] for colour in range(3)]
    base = [scale * transfer[colour] + slope[colour] for colour in range(3)]

    @pl.loop(0, height // ROWS)
    def _(chunk):
        at = pl.ds(pl.multiple_of(chunk * ROWS, ROWS), ROWS)
        white = tinted = log = jnp.zeros((ROWS, 2 * LANES), jnp.float32)
        for front in range(4):
            phase = (chip + 3 - front) % 4
            own = phase == 3
            slot = phase % 3
            part = [
                jnp.where(own, res[7, plane, at, :], parts[slot, plane, at, :])
                for plane in range(3)
            ]
            through = jnp.exp2(log * density)
            white = white + through * part[0]
            tinted = tinted + through * part[1]
            log = log + part[2]
        for colour in range(3):
            final[colour, at, :] = base[colour] * white + slope[colour] * tinted
        bend = jnp.tanh(log * (density * (-0.5 * LN2)))
        final[3, at, :] = 2.0 * bend / (1.0 + bend)

    out = pltpu.make_async_copy(final, image, out_sem)
    out.start()
    for phase in range(4):
        to_sibling(phase).wait_send()
    for phase in range(3):
        to_owner(phase).wait_send()
    for kind in range(4):

        @pl.when(can_send[kind])
        def _(kind=kind):
            @pl.loop(0, 16)
            def _(tile):
                halo(kind, tile).wait_send()

    out.wait()


def on_device(volume, transfer):
    slices, height, columns = volume.shape
    own = columns // lax.axis_size("depth")
    f32 = jnp.float32
    dma = pltpu.SemaphoreType.DMA
    return pl.pallas_call(
        kernel,
        out_shape=jax.ShapeDtypeStruct((4, height, own), f32),
        in_specs=[
            pl.BlockSpec(memory_space=pltpu.SMEM),
            pl.BlockSpec(memory_space=pl.ANY),
        ],
        out_specs=pl.BlockSpec(memory_space=pl.ANY),
        scratch_shapes=[
            pltpu.VMEM((18, slices + 2, height + 16, LANES), f32),
            pltpu.VMEM((8, 3, height, own), f32),
            pltpu.VMEM((4, 3, height, own), f32),
            pltpu.VMEM((3, 3, height, own), f32),
            pltpu.VMEM((4, height, own), f32),
            dma((16,)),
            dma((4, 16)),
            dma((4, 16)),
            dma((4,)),
            dma((4,)),
            dma((3,)),
            dma((3,)),
            dma,
        ],
        compiler_params=pltpu.CompilerParams(
            collective_id=0, has_side_effects=True, vmem_limit_bytes=56 * 1024 * 1024
        ),
        name="render",
    )(transfer, volume)


def solution(mesh):
    in_specs = (P("depth", "row", None), P())
    out_specs = P(None, "row", "depth")
    return jax.shard_map(
        on_device, mesh=mesh, in_specs=in_specs, out_specs=out_specs, check_vma=False
    )
```

time: 484 us -> 42.9 us (0.09)
  other arithmetic: 327 us -> 0 us
  local copies, waits for them, and re-layouts: 91.7 us -> 1.67 us
  Pallas kernels: 0 us -> 41 us
  blocking collectives: 36.3 us -> 0 us
  starting transfers between devices: 11.3 us -> 0 us
  waiting for transfers between devices: 9.72 us -> 0 us
    another operation x19 -> x0, other arithmetic: 262 us -> none  [the longest x12 172 us: emit(): jnp.stack([(transfer[channel] + transfer[3 + channel] * tinting) * weight...]
    slice x15 -> x0, local copies, waits for them, and re-layouts: 56.4 us -> none  [the longest x6 49.7 us: slope_cols(): right = jnp.concatenate([center[..., 1:], zero_col], -1)]
    pallas_call x0 -> x1, Pallas kernels: none -> 41 us  [on_device(): pl.pallas_call(kernel, out_shape=jax.ShapeDtypeStruct((4, height, own), f...]
    all_to_all x1 -> x0, blocking collectives: 36.3 us -> none  [on_device(): lax.all_to_all(partial_image[None], 'depth', split_axis=3, concat_axis=0,...]
    reduce_sum x7 -> x0, other arithmetic: 27.1 us -> none  [the longest x6 23.7 us: march(): color = color + jnp.sum(passing[None] * emitted, 1)]
    unnamed x8 -> x1, local copies, waits for them, and re-layouts: 27 us -> 1.67 us
    concatenate x2 -> x0, other arithmetic: 20.9 us -> none  [the longest x1 20.7 us: with_halo(): jnp.concatenate([lax.ppermute(tail, axis, [(i, (i + 1) % count) for i in...]
    ppermute x4 -> x0, starting transfers between devices: 11.3 us -> none  [the longest x2 8.08 us: with_halo(): lax.ppermute(tail, axis, [(i, (i + 1) % count) for i in range(ends)])]
  transfers between devices with their start and end apart: 4 -> 0, of which waited for: 2 -> 0; matrix products, arithmetic and copies ran while one was open for 2% -> 0% of each run, Pallas kernels for 0% -> 0%
where the time goes in v1:
time: 42.9 us; the launch traced here: 42.7 us
  Pallas kernels  41 us (96%)
  local copies, waits for them, and re-layouts  1.67 us (4%)
    pallas_call x1, Pallas kernels, on_device(): pl.pallas_call(kernel, out_shape=jax.ShapeDtypeStruct((4, height, own), f...  41 us
    unnamed x1, local copies, waits for them, and re-layouts  1.67 us

profile of v1, /device:TPU:1, one launch (start us, length us, event | category | flops | bytes accessed | tf_op | source)
XLA Modules:
  0.0 42.7 jit_solution(5130824145394002447)
XLA Ops:
  0.0 41.0 %render.1 = f32[4,64,256]{2,1,0:T(8,128)} custom-call(f32[8]{0:T(128)} %transfer.1, f32[48,64,2048]{2,1,0:T(8,128)} %volume.1), custom_call_target="tpu_custom_call" | custom-call | tf_op jit(solution)/shard_map/render/pallas_call | solution.py:325
  41.0 1.7 %copy.4 = f32[4,64,256]{2,1,0:T(8,128)} copy(f32[4,64,256]{2,1,0:T(8,128)} %render.1) | data formatting | bytes 524288

commit v2 on v1

--- a/solution.py
+++ b/solution.py
@@ -10,6 +10,7 @@
 LANES = 128
 ROWS = 16
 TOP = 8
+EARLY = 5
 MESH = pl.DeviceIdType.MESH
 
 
@@ -28,7 +29,6 @@
     res,
     sib,
     parts,
-    final,
     load_sem,
     halo_send,
     halo_recv,
@@ -36,7 +36,6 @@
     sib_recv,
     part_send,
     part_recv,
-    out_sem,
 ):
     depth, row = lax.axis_index("depth"), lax.axis_index("row")
     depths, rows = lax.axis_size("depth"), lax.axis_size("row")
@@ -56,9 +55,7 @@
     lead = 2 - 2 * core
     order = [lead, lead + 1, lead + 15, lead + 2]
     second = [3 * core, 15 + 5 * core]
-    for position in order + second:
-        load(position).start()
-    for position in range(5, 15):
+    for position in order:
         load(position).start()
 
     def partners(act):
@@ -92,8 +89,7 @@
     def clear_row(at):
         @pl.loop(0, 16)
         def _(tile):
-            @pl.loop(0, slices)
-            def _(z):
+            for z in range(slices):
                 vol[tile + 1, z + 1, pl.ds(at, 1), :] = jnp.zeros((1, LANES), jnp.float32)
 
     pl.when(depth == 0)(lambda: clear_slab(0))
@@ -103,7 +99,6 @@
 
     count = 3 + (depth > 0).astype(jnp.int32) + (depth < depths - 1).astype(jnp.int32)
     count = count + (row > 0).astype(jnp.int32) + (row < rows - 1).astype(jnp.int32)
-    pl.semaphore_wait(barrier, count)
 
     def halo(kind, tile):
         columns = pl.ds(pl.multiple_of(tile * LANES, LANES), LANES)
@@ -120,8 +115,8 @@
         return pltpu.make_async_remote_copy(
             src_ref=source,
             dst_ref=target,
-            send_sem=halo_send.at[kind, tile],
-            recv_sem=halo_recv.at[kind, tile],
+            send_sem=halo_send.at[kind],
+            recv_sem=halo_recv.at[kind, tile // 2],
             device_id=device,
             device_id_type=MESH,
         )
@@ -139,15 +134,19 @@
                     halo(kind, 2 * block + side).start()
 
     def receive_halos(kinds, block):
+        tiles = pl.ds(2 * block + 1, 2)
+        landed = (
+            vol.at[tiles, 0, pl.ds(TOP, height), :],
+            vol.at[tiles, slices + 1, pl.ds(TOP, height), :],
+            vol.at[tiles, pl.ds(1, slices), pl.ds(TOP - 1, 1), :],
+            vol.at[tiles, pl.ds(1, slices), pl.ds(TOP + height, 1), :],
+        )
         for kind in kinds:
 
             @pl.when(can_receive[kind])
             def _(kind=kind):
-                for side in range(2):
-                    halo(kind, 2 * block + side).wait_recv()
-
-    send_halos(0)
-    send_halos(1)
+                both = landed[kind]
+                pltpu.make_async_copy(both, both, halo_recv.at[kind, block]).wait()
 
     density = transfer[6] * (2.0 / (slices * depths))
     ambient = 0.5 * transfer[7]
@@ -155,47 +154,86 @@
     lane = lax.broadcasted_iota(jnp.int32, (ROWS, LANES), 1)
     lowest, highest = lane == 0, lane == LANES - 1
 
-    def march(tile, start, step):
-        here = pl.ds(pl.multiple_of(TOP + start, 8), ROWS)
-        above, below = pl.ds(TOP + start - 1, ROWS), pl.ds(TOP + start + 1, ROWS)
+    def shade(tile, z, here, above, below, ahead, middle, behind, side):
+        value = middle[side]
+        if side == 0:
+            before, after = vol[tile, z + 1, here, :], middle[1]
+        else:
+            before, after = middle[0], vol[tile + 3, z + 1, here, :]
+        left = pltpu.roll(jnp.where(highest, before, value), 1, 1)
+        right = pltpu.roll(jnp.where(lowest, after, value), LANES - 1, 1)
+        by_depth = behind - ahead
+        by_row = vol[tile + 1 + side, z + 1, below, :] - vol[tile + 1 + side, z + 1, above, :]
+        by_column = right - left
+        plane = by_row + by_column
+        along = by_depth + (plane + plane)
+        square = (by_depth * by_depth + 4.0) + (by_row * by_row + by_column * by_column)
+        return jnp.abs(along) * lax.rsqrt(square)
+
+    def around(start):
+        return tuple(pl.ds(TOP + start + shift, ROWS) for shift in (0, -1, 1))
+
+    def march(tile, start, step, ends):
+        here, above, below = around(start)
+
+        def cells(slab):
+            return tuple(vol[tile + 1 + side, slab, here, :] for side in range(2))
+
+        def absorb(middle, side, log):
+            log = log - jnp.log2(1.0 + jnp.exp2(middle[side] * LOG2E))
+            return log, jnp.exp2(log * density)
 
         def slab(z, carry):
             ahead, middle, logs, passing, white, tinted = carry
-            behind = tuple(vol[tile + 1 + side, z + 2, here, :] for side in range(2))
-            outer = (vol[tile, z + 1, here, :], vol[tile + 3, z + 1, here, :])
-            lefts, rights = (outer[0], middle[0]), (middle[1], outer[1])
+            behind = cells(z + 2)
             out = []
             for side in range(2):
-                value = middle[side]
-                left = pltpu.roll(jnp.where(highest, lefts[side], value), 1, 1)
-                right = pltpu.roll(jnp.where(lowest, rights[side], value), LANES - 1, 1)
-                by_depth = behind[side] - ahead[side]
-                by_row = vol[tile + 1 + side, z + 1, below, :] - vol[tile + 1 + side, z + 1, above, :]
-                by_column = right - left
-                plane = by_row + by_column
-                along = by_depth + (plane + plane)
-                square = (by_depth * by_depth + 4.0) + (by_row * by_row + by_column * by_column)
-                lambert = jnp.abs(along) * lax.rsqrt(square)
-                log = logs[side] - jnp.log2(1.0 + jnp.exp2(value * LOG2E))
-                after = jnp.exp2(log * density)
+                lambert = shade(tile, z, here, above, below, ahead[side], middle, behind[side], side)
+                log, after = absorb(middle, side, logs[side])
                 lit = (passing[side] - after) * (lambert + lift)
-                out.append(
-                    (log, after, white[side] + lit, tinted[side] + lit * jnp.tanh(value))
-                )
+                tint = jnp.tanh(middle[side])
+                out.append((log, after, white[side] + lit, tinted[side] + lit * tint))
             return (middle, behind) + tuple(zip(*out))
 
         zero = jnp.zeros((ROWS, LANES), jnp.float32)
-        carry = tuple(
-            tuple(vol[tile + 1 + side, z, here, :] for side in range(2)) for z in range(2)
-        )
-        carry = carry + ((zero,) * 2, (zero + 1.0,) * 2, (zero,) * 2, (zero,) * 2)
-        _, _, logs, _, white, tinted = lax.fori_loop(0, slices, slab, carry, unroll=True)
+        if ends:
+            carry = (cells(0), cells(1), (zero,) * 2, (zero + 1.0,) * 2, (zero,) * 2, (zero,) * 2)
+            _, _, logs, _, white, tinted = lax.fori_loop(0, slices, slab, carry, unroll=True)
+        else:
+            middle = cells(1)
+            logs, passing = zip(*(absorb(middle, side, zero) for side in range(2)))
+            carry = (middle, cells(2), logs, passing, (zero,) * 2, (zero,) * 2)
+            carry = lax.fori_loop(1, slices - 1, slab, carry, unroll=True)
+            _, middle, logs, _, white, tinted = carry
+            logs = tuple(absorb(middle, side, logs[side])[0] for side in range(2))
         put = pl.ds(pl.multiple_of(start, 8), ROWS)
         for side in range(2):
             columns = pl.ds(side * LANES, LANES)
             res[step, 0, put, columns] = white[side]
             res[step, 1, put, columns] = tinted[side]
             res[step, 2, put, columns] = logs[side]
+
+    def add_ends(tile, start, step):
+        here, above, below = around(start)
+        put = pl.ds(pl.multiple_of(start, 8), ROWS)
+        for z in (0, slices - 1):
+            ahead, middle, behind = (
+                tuple(vol[tile + 1 + side, z + shift, here, :] for side in range(2))
+                for shift in range(3)
+            )
+            for side in range(2):
+                columns = pl.ds(side * LANES, LANES)
+                value = middle[side]
+                lambert = shade(tile, z, here, above, below, ahead[side], middle, behind[side], side)
+                own = jnp.log2(1.0 + jnp.exp2(value * LOG2E))
+                if z == 0:
+                    passed = 1.0 - jnp.exp2(own * -density)
+                else:
+                    log = res[step, 2, put, columns]
+                    passed = jnp.exp2((log + own) * density) - jnp.exp2(log * density)
+                lit = passed * (lambert + lift)
+                res[step, 0, put, columns] += lit
+                res[step, 1, put, columns] += lit * jnp.tanh(value)
 
     def to_sibling(phase):
         return pltpu.make_async_remote_copy(
@@ -230,43 +268,74 @@
             res[2 * phase + 1, 1, at, :] = front[1] + through * back[1]
             res[2 * phase + 1, 2, at, :] = front[2] + back[2]
 
-    @pl.loop(0, 8)
-    def _(step):
-        block = block_of(depth, step)
-        phase, half = step // 2, step % 2
-        pl.when(step < 6)(lambda: send_halos(step + 2))
-
+    def wait_loads(step):
         @pl.when(step == 0)
         def _():
             for position in order:
                 load(position).wait()
+            for position in second:
+                load(position).start()
+            for position in range(5, 15):
+                load(position).start()
 
         @pl.when(step == 1)
         def _():
             for position in second:
                 load(position).wait()
 
-        @pl.when((half == 0) & (step >= 2) & (step < 6))
+        @pl.when((step == 2) | (step == 4))
         def _():
             for position in range(1, 5):
-                load(4 * phase + position).wait()
+                load(2 * step + position).wait()
 
         @pl.when(step == 6)
         def _():
             for position in range(13, 15):
                 load(position).wait()
 
-        receive_halos((0, 1), block)
-
-        @pl.loop(0, 2)
-        def _(turn):
-            pl.when(turn == 1)(lambda: receive_halos((2, 3), block))
-            march(2 * block, ROWS * (1 - turn), step)
-            march(2 * block, ROWS * (2 + turn), step)
-
-        pl.when(half == 0)(lambda: to_sibling(phase).start())
-
-        @pl.when(half == 1)
+    @pl.loop(0, EARLY)
+    def _(step):
+        wait_loads(step)
+
+        @pl.when(step == 1)
+        def _():
+            pl.semaphore_wait(barrier, count)
+
+        @pl.when(step > 0)
+        def _():
+            send_halos(2 * step - 2)
+            send_halos(2 * step - 1)
+
+        block = block_of(depth, step)
+        march(2 * block, ROWS, step, False)
+        march(2 * block, 2 * ROWS, step, False)
+
+    @pl.loop(0, 16 - EARLY)
+    def _(index):
+        late = jnp.maximum(index - EARLY, 0)
+        step = jnp.where(index < EARLY, index, EARLY + late // 2)
+        turn = jnp.where(index < EARLY, 1, late % 2)
+        phase, half = step // 2, step % 2
+        block = block_of(depth, step)
+
+        @pl.when(turn == 0)
+        def _():
+            wait_loads(step)
+            receive_halos((0, 1), block)
+
+        @pl.when(index < EARLY)
+        def _():
+            receive_halos((0, 1), block)
+            add_ends(2 * block, ROWS, step)
+            add_ends(2 * block, 2 * ROWS, step)
+
+        pl.when(turn == 1)(lambda: receive_halos((2, 3), block))
+        march(2 * block, ROWS * (1 - turn), step, True)
+        march(2 * block, ROWS * (2 + turn), step, True)
+
+        pl.when((turn == 1) & (half == 0))(lambda: to_sibling(phase).start())
+
+        @pl.when((turn == 1) & (half == 1))
         def _():
             to_sibling(phase).wait_recv()
             join(phase)
@@ -296,12 +365,10 @@
             tinted = tinted + through * part[1]
             log = log + part[2]
         for colour in range(3):
-            final[colour, at, :] = base[colour] * white + slope[colour] * tinted
+            image[colour, at, :] = base[colour] * white + slope[colour] * tinted
         bend = jnp.tanh(log * (density * (-0.5 * LN2)))
-        final[3, at, :] = 2.0 * bend / (1.0 + bend)
-
-    out = pltpu.make_async_copy(final, image, out_sem)
-    out.start()
+        image[3, at, :] = 2.0 * bend / (1.0 + bend)
+
     for phase in range(4):
         to_sibling(phase).wait_send()
     for phase in range(3):
@@ -310,11 +377,8 @@
 
         @pl.when(can_send[kind])
         def _(kind=kind):
-            @pl.loop(0, 16)
-            def _(tile):
-                halo(kind, tile).wait_send()
-
-    out.wait()
+            sent = volume.at[0] if kind < 2 else volume.at[:, pl.ds(0, 1), :]
+            pltpu.make_async_copy(sent, sent, halo_send.at[kind]).wait()
 
 
 def on_device(volume, transfer):
@@ -324,26 +388,24 @@
     dma = pltpu.SemaphoreType.DMA
     return pl.pallas_call(
         kernel,
-        out_shape=jax.ShapeDtypeStruct((4, height, own), f32),
+        out_shape=pltpu.VMEM((4, height, own), f32),
         in_specs=[
             pl.BlockSpec(memory_space=pltpu.SMEM),
             pl.BlockSpec(memory_space=pl.ANY),
         ],
-        out_specs=pl.BlockSpec(memory_space=pl.ANY),
+        out_specs=pl.BlockSpec(memory_space=pltpu.VMEM),
         scratch_shapes=[
             pltpu.VMEM((18, slices + 2, height + 16, LANES), f32),
             pltpu.VMEM((8, 3, height, own), f32),
             pltpu.VMEM((4, 3, height, own), f32),
             pltpu.VMEM((3, 3, height, own), f32),
-            pltpu.VMEM((4, height, own), f32),
             dma((16,)),
-            dma((4, 16)),
-            dma((4, 16)),
+            dma((4,)),
+            dma((4, 8)),
             dma((4,)),
             dma((4,)),
             dma((3,)),
             dma((3,)),
-            dma,
         ],
         compiler_params=pltpu.CompilerParams(
             collective_id=0, has_side_effects=True, vmem_limit_bytes=56 * 1024 * 1024

time: 42.9 us -> 34.1 us (0.79)
  Pallas kernels: 41 us -> 33.2 us
  local copies, waits for them, and re-layouts: 1.67 us -> 0.71 us
    pallas_call x1, Pallas kernels: 41 us -> 33.2 us  [on_device(): pl.pallas_call(kernel, out_shape=pltpu.VMEM((4, height, own), f32), in_sp...]
    unnamed x1, local copies, waits for them, and re-layouts: 1.67 us -> 0.71 us
where the time goes in v2:
time: 34.1 us; the launch traced here: 33.9 us
  Pallas kernels  33.2 us (97%)
  local copies, waits for them, and re-layouts  0.71 us (2%)
    pallas_call x1, Pallas kernels, on_device(): pl.pallas_call(kernel, out_shape=pltpu.VMEM((4, height, own), f32), in_sp...  33.2 us
    unnamed x1, local copies, waits for them, and re-layouts  0.71 us

profile of v2, /device:TPU:1, one launch (start us, length us, event | category | flops | bytes accessed | tf_op | source)
XLA Modules:
  0.0 33.9 jit_solution(11559608820981043136)
XLA Ops:
  0.0 33.2 %render.1 = f32[4,64,256]{2,1,0:T(8,128)S(1)} custom-call(f32[8]{0:T(128)} %transfer.1, f32[48,64,2048]{2,1,0:T(8,128)} %volume.1), custom_call_target="tpu_custom_call" | custom-call | tf_op jit(solution)/shard_map/render/pallas_call | solution.py:389
  33.2 0.7 %copy.4 = f32[4,64,256]{2,1,0:T(8,128)} copy(f32[4,64,256]{2,1,0:T(8,128)S(1)} %render.1) | data formatting | bytes 524288

commit v3 on v2

--- a/solution.py
+++ b/solution.py
@@ -14,11 +14,15 @@
 MESH = pl.DeviceIdType.MESH
 
 
+def ahead_of(phase):
+    return jnp.where(phase == 0, 2, jnp.where(phase == 1, 1, jnp.where(phase == 2, 3, 0)))
+
+
 def block_of(depth, step):
     chip, core = depth // 2, depth % 2
     phase, half = step // 2, step % 2
     parity = core * half + (1 - core) * (1 - half)
-    return 2 * ((chip + 1 + phase) % 4) + parity
+    return 2 * ((chip + ahead_of(phase)) % 4) + parity
 
 
 def kernel(
@@ -26,6 +30,7 @@
     volume,
     image,
     vol,
+    slabs,
     res,
     sib,
     parts,
@@ -42,7 +47,7 @@
     slices, height, _ = volume.shape
     chip, core = depth // 2, depth % 2
     sibling = depth + 1 - 2 * core
-    first = 4 * ((chip + 1) % 4)
+    first = 4 * ((chip + 2) % 4)
 
     def load(position):
         tile = (first + position) % 16
@@ -55,7 +60,7 @@
     lead = 2 - 2 * core
     order = [lead, lead + 1, lead + 15, lead + 2]
     second = [3 * core, 15 + 5 * core]
-    for position in order:
+    for position in order + second:
         load(position).start()
 
     def partners(act):
@@ -81,10 +86,8 @@
         vol[0, z + 1, pl.ds(TOP, height), :] = jnp.zeros((height, LANES), jnp.float32)
         vol[17, z + 1, pl.ds(TOP, height), :] = jnp.zeros((height, LANES), jnp.float32)
 
-    def clear_slab(slab):
-        @pl.loop(0, 16)
-        def _(tile):
-            vol[tile + 1, slab, pl.ds(TOP, height), :] = jnp.zeros((height, LANES), jnp.float32)
+    def clear_slab(kind):
+        slabs[kind] = jnp.zeros((height, 16 * LANES), jnp.float32)
 
     def clear_row(at):
         @pl.loop(0, 16)
@@ -93,30 +96,30 @@
                 vol[tile + 1, z + 1, pl.ds(at, 1), :] = jnp.zeros((1, LANES), jnp.float32)
 
     pl.when(depth == 0)(lambda: clear_slab(0))
-    pl.when(depth == depths - 1)(lambda: clear_slab(slices + 1))
+    pl.when(depth == depths - 1)(lambda: clear_slab(1))
     pl.when(row == 0)(lambda: clear_row(TOP - 1))
     pl.when(row == rows - 1)(lambda: clear_row(TOP + height))
 
     count = 3 + (depth > 0).astype(jnp.int32) + (depth < depths - 1).astype(jnp.int32)
     count = count + (row > 0).astype(jnp.int32) + (row < rows - 1).astype(jnp.int32)
 
-    def halo(kind, tile):
-        columns = pl.ds(pl.multiple_of(tile * LANES, LANES), LANES)
+    def halo(kind, group):
         if kind < 2:
+            columns = pl.ds(pl.multiple_of(group * 4 * LANES, 4 * LANES), 4 * LANES)
             source = volume.at[slices - 1 if kind == 0 else 0, :, columns]
-            target = vol.at[tile + 1, 0 if kind == 0 else slices + 1, pl.ds(TOP, height), :]
+            target = slabs.at[kind, :, columns]
             device = {"depth": depth + 1 if kind == 0 else depth - 1}
         else:
-            source = volume.at[:, pl.ds(height - 1 if kind == 2 else 0, 1), columns]
-            target = vol.at[
-                tile + 1, pl.ds(1, slices), pl.ds(TOP - 1 if kind == 2 else TOP + height, 1), :
-            ]
+            tiles = pl.ds(4 * group + 1, 4)
+            last, beyond = (TOP + height - 1, TOP - 1) if kind == 2 else (TOP, TOP + height)
+            source = vol.at[tiles, pl.ds(1, slices), pl.ds(last, 1), :]
+            target = vol.at[tiles, pl.ds(1, slices), pl.ds(beyond, 1), :]
             device = {"row": row + 1 if kind == 2 else row - 1}
         return pltpu.make_async_remote_copy(
             src_ref=source,
             dst_ref=target,
             send_sem=halo_send.at[kind],
-            recv_sem=halo_recv.at[kind, tile // 2],
+            recv_sem=halo_recv.at[kind, group],
             device_id=device,
             device_id_type=MESH,
         )
@@ -124,29 +127,22 @@
     can_send = (depth < depths - 1, depth > 0, row < rows - 1, row > 0)
     can_receive = (depth > 0, depth < depths - 1, row > 0, row < rows - 1)
 
-    def send_halos(step):
-        for kind, to in ((0, depth + 1), (1, depth - 1), (2, depth), (3, depth)):
+    def group_of(depth, phase):
+        return (depth // 2 + ahead_of(phase)) % 4
+
+    def send_halos(kinds, phase):
+        for kind in kinds:
 
             @pl.when(can_send[kind])
-            def _(kind=kind, to=to):
-                block = block_of(to, step)
-                for side in range(2):
-                    halo(kind, 2 * block + side).start()
-
-    def receive_halos(kinds, block):
-        tiles = pl.ds(2 * block + 1, 2)
-        landed = (
-            vol.at[tiles, 0, pl.ds(TOP, height), :],
-            vol.at[tiles, slices + 1, pl.ds(TOP, height), :],
-            vol.at[tiles, pl.ds(1, slices), pl.ds(TOP - 1, 1), :],
-            vol.at[tiles, pl.ds(1, slices), pl.ds(TOP + height, 1), :],
-        )
+            def _(kind=kind):
+                halo(kind, group_of((depth + 1, depth - 1, depth, depth)[kind], phase)).start()
+
+    def receive_halos(kinds, phase):
         for kind in kinds:
 
             @pl.when(can_receive[kind])
             def _(kind=kind):
-                both = landed[kind]
-                pltpu.make_async_copy(both, both, halo_recv.at[kind, block]).wait()
+                halo(kind, group_of(depth, phase)).wait_recv()
 
     density = transfer[6] * (2.0 / (slices * depths))
     ambient = 0.5 * transfer[7]
@@ -173,19 +169,26 @@
     def around(start):
         return tuple(pl.ds(TOP + start + shift, ROWS) for shift in (0, -1, 1))
 
+    def outside(tile, start):
+        put = pl.ds(pl.multiple_of(start, 8), ROWS)
+        columns = [pl.ds(pl.multiple_of((tile + side) * LANES, LANES), LANES) for side in range(2)]
+        return [lambda kind=kind: tuple(slabs[kind, put, column] for column in columns) for kind in range(2)]
+
     def march(tile, start, step, ends):
         here, above, below = around(start)
 
         def cells(slab):
             return tuple(vol[tile + 1 + side, slab, here, :] for side in range(2))
+
+        first, last = outside(tile, start)
 
         def absorb(middle, side, log):
             log = log - jnp.log2(1.0 + jnp.exp2(middle[side] * LOG2E))
             return log, jnp.exp2(log * density)
 
-        def slab(z, carry):
+        def slab(z, carry, behind=None):
             ahead, middle, logs, passing, white, tinted = carry
-            behind = cells(z + 2)
+            behind = cells(z + 2) if behind is None else behind
             out = []
             for side in range(2):
                 lambert = shade(tile, z, here, above, below, ahead[side], middle, behind[side], side)
@@ -197,8 +200,9 @@
 
         zero = jnp.zeros((ROWS, LANES), jnp.float32)
         if ends:
-            carry = (cells(0), cells(1), (zero,) * 2, (zero + 1.0,) * 2, (zero,) * 2, (zero,) * 2)
-            _, _, logs, _, white, tinted = lax.fori_loop(0, slices, slab, carry, unroll=True)
+            carry = (first(), cells(1), (zero,) * 2, (zero + 1.0,) * 2, (zero,) * 2, (zero,) * 2)
+            carry = lax.fori_loop(0, slices - 1, slab, carry, unroll=True)
+            _, _, logs, _, white, tinted = slab(slices - 1, carry, last())
         else:
             middle = cells(1)
             logs, passing = zip(*(absorb(middle, side, zero) for side in range(2)))
@@ -216,11 +220,13 @@
     def add_ends(tile, start, step):
         here, above, below = around(start)
         put = pl.ds(pl.multiple_of(start, 8), ROWS)
+        first, last = outside(tile, start)
         for z in (0, slices - 1):
             ahead, middle, behind = (
                 tuple(vol[tile + 1 + side, z + shift, here, :] for side in range(2))
                 for shift in range(3)
             )
+            ahead, behind = (first(), behind) if z == 0 else (ahead, last())
             for side in range(2):
                 columns = pl.ds(side * LANES, LANES)
                 value = middle[side]
@@ -245,19 +251,21 @@
             device_id_type=MESH,
         )
 
-    def to_owner(phase):
+    pieces = ((2, ROWS, 2 * ROWS), (3, 0, ROWS), (4, 3 * ROWS, ROWS))
+
+    def to_owner(phase, number, low, count):
+        span = pl.ds(low, count)
         return pltpu.make_async_remote_copy(
-            src_ref=res.at[2 * phase + 1],
-            dst_ref=parts.at[phase],
-            send_sem=part_send.at[phase],
-            recv_sem=part_recv.at[phase],
-            device_id={"depth": 2 * ((chip + 1 + phase) % 4) + core},
+            src_ref=res.at[2 * phase + 1, :, span, :],
+            dst_ref=parts.at[phase, :, span, :],
+            send_sem=part_send.at[number],
+            recv_sem=part_recv.at[number],
+            device_id={"depth": 2 * ((chip + ahead_of(phase)) % 4) + core},
             device_id_type=MESH,
         )
 
-    def join(phase):
-        @pl.loop(0, height // ROWS)
-        def _(chunk):
+    def join(phase, chunks):
+        for chunk in chunks:
             at = pl.ds(pl.multiple_of(chunk * ROWS, ROWS), ROWS)
             mine = [res[2 * phase + 1, plane, at, :] for plane in range(3)]
             other = [sib[phase, plane, at, :] for plane in range(3)]
@@ -273,24 +281,24 @@
         def _():
             for position in order:
                 load(position).wait()
-            for position in second:
+            for position in range(11, 15):
                 load(position).start()
-            for position in range(5, 15):
+
+        @pl.when(step == 1)
+        def _():
+            for position in range(5, 11):
                 load(position).start()
-
-        @pl.when(step == 1)
-        def _():
             for position in second:
                 load(position).wait()
 
-        @pl.when((step == 2) | (step == 4))
-        def _():
-            for position in range(1, 5):
-                load(2 * step + position).wait()
-
-        @pl.when(step == 6)
-        def _():
-            for position in range(13, 15):
+        @pl.when(step == 2)
+        def _():
+            for position in range(11, 15):
+                load(position).wait()
+
+        @pl.when(step == 4)
+        def _():
+            for position in range(5, 11):
                 load(position).wait()
 
     @pl.loop(0, EARLY)
@@ -300,62 +308,86 @@
         @pl.when(step == 1)
         def _():
             pl.semaphore_wait(barrier, count)
-
-        @pl.when(step > 0)
-        def _():
-            send_halos(2 * step - 2)
-            send_halos(2 * step - 1)
+            send_halos((0, 1, 2, 3), 0)
+            send_halos((0, 1), 1)
+
+        @pl.when(step == 2)
+        def _():
+            send_halos((2, 3), 1)
+            send_halos((0, 1), 2)
+            send_halos((0, 1), 3)
+
+        @pl.when(step == 4)
+        def _():
+            send_halos((2, 3), 2)
+            send_halos((2, 3), 3)
 
         block = block_of(depth, step)
         march(2 * block, ROWS, step, False)
         march(2 * block, 2 * ROWS, step, False)
 
-    @pl.loop(0, 16 - EARLY)
+    def finish(step, turn):
+        phase, half = step // 2, step % 2
+        early = step < EARLY
+        pl.when((half == 0) & (turn == 1))(lambda: to_sibling(phase).start())
+
+        @pl.when((half == 1) & (early | (turn == 0)))
+        def _():
+            to_sibling(phase).wait_recv()
+
+        @pl.when((half == 1) & early)
+        def _():
+            join(phase, range(4))
+            to_owner(phase, phase, 0, height).start()
+
+        @pl.when((half == 1) & (step >= EARLY))
+        def _():
+            join(phase, (1 - turn, 2 + turn))
+
+        @pl.when((step == 5) & (turn == 0))
+        def _():
+            to_owner(2, *pieces[0]).start()
+
+        @pl.when((step == 5) & (turn == 1))
+        def _():
+            to_owner(2, *pieces[1]).start()
+            to_owner(2, *pieces[2]).start()
+
+    @pl.loop(0, EARLY)
+    def _(step):
+        pl.when(step % 2 == 0)(lambda: receive_halos((0, 1, 2, 3), step // 2))
+        block = block_of(depth, step)
+        add_ends(2 * block, ROWS, step)
+        add_ends(2 * block, 2 * ROWS, step)
+        march(2 * block, 0, step, True)
+        march(2 * block, 3 * ROWS, step, True)
+        finish(step, 1)
+
+    @pl.loop(0, 2 * (8 - EARLY))
     def _(index):
-        late = jnp.maximum(index - EARLY, 0)
-        step = jnp.where(index < EARLY, index, EARLY + late // 2)
-        turn = jnp.where(index < EARLY, 1, late % 2)
-        phase, half = step // 2, step % 2
+        step, turn = EARLY + index // 2, index % 2
+        pl.when((step % 2 == 0) & (turn == 0))(lambda: receive_halos((0, 1, 2, 3), step // 2))
         block = block_of(depth, step)
-
-        @pl.when(turn == 0)
-        def _():
-            wait_loads(step)
-            receive_halos((0, 1), block)
-
-        @pl.when(index < EARLY)
-        def _():
-            receive_halos((0, 1), block)
-            add_ends(2 * block, ROWS, step)
-            add_ends(2 * block, 2 * ROWS, step)
-
-        pl.when(turn == 1)(lambda: receive_halos((2, 3), block))
         march(2 * block, ROWS * (1 - turn), step, True)
         march(2 * block, ROWS * (2 + turn), step, True)
-
-        pl.when((turn == 1) & (half == 0))(lambda: to_sibling(phase).start())
-
-        @pl.when((turn == 1) & (half == 1))
-        def _():
-            to_sibling(phase).wait_recv()
-            join(phase)
-            pl.when(phase < 3)(lambda: to_owner(phase).start())
-
-    for phase in range(3):
-        to_owner(phase).wait_recv()
+        finish(step, turn)
+
+    sends = ((0, 0, 0, height), (1, 1, 0, height)) + tuple((2,) + piece for piece in pieces)
+    for send in sends:
+        to_owner(*send).wait_recv()
 
     scale = (1.0 - ambient) / 3.0
     slope = [scale * 0.5 * transfer[3 + colour] for colour in range(3)]
     base = [scale * transfer[colour] + slope[colour] for colour in range(3)]
 
-    @pl.loop(0, height // ROWS)
+    @pl.loop(0, height // ROWS, unroll=True)
     def _(chunk):
         at = pl.ds(pl.multiple_of(chunk * ROWS, ROWS), ROWS)
         white = tinted = log = jnp.zeros((ROWS, 2 * LANES), jnp.float32)
         for front in range(4):
-            phase = (chip + 3 - front) % 4
-            own = phase == 3
-            slot = phase % 3
+            ahead = (chip + 4 - front) % 4
+            own = ahead == 0
+            slot = jnp.where(ahead == 2, 0, jnp.where(ahead == 3, 2, 1))
             part = [
                 jnp.where(own, res[7, plane, at, :], parts[slot, plane, at, :])
                 for plane in range(3)
@@ -371,13 +403,13 @@
 
     for phase in range(4):
         to_sibling(phase).wait_send()
-    for phase in range(3):
-        to_owner(phase).wait_send()
+    for send in sends:
+        to_owner(*send).wait_send()
     for kind in range(4):
 
         @pl.when(can_send[kind])
         def _(kind=kind):
-            sent = volume.at[0] if kind < 2 else volume.at[:, pl.ds(0, 1), :]
+            sent = slabs.at[0] if kind < 2 else vol.at[pl.ds(1, 16), pl.ds(1, slices), pl.ds(TOP, 1), :]
             pltpu.make_async_copy(sent, sent, halo_send.at[kind]).wait()
 
 
@@ -396,16 +428,17 @@
         out_specs=pl.BlockSpec(memory_space=pltpu.VMEM),
         scratch_shapes=[
             pltpu.VMEM((18, slices + 2, height + 16, LANES), f32),
+            pltpu.VMEM((2, height, columns), f32),
             pltpu.VMEM((8, 3, height, own), f32),
             pltpu.VMEM((4, 3, height, own), f32),
             pltpu.VMEM((3, 3, height, own), f32),
             dma((16,)),
             dma((4,)),
-            dma((4, 8)),
+            dma((4, 4)),
             dma((4,)),
             dma((4,)),
-            dma((3,)),
-            dma((3,)),
+            dma((5,)),
+            dma((5,)),
         ],
         compiler_params=pltpu.CompilerParams(
             collective_id=0, has_side_effects=True, vmem_limit_bytes=56 * 1024 * 1024

time: 34.1 us -> 33 us (0.968)
  Pallas kernels: 33.2 us -> 32.1 us
    pallas_call x1, Pallas kernels: 33.2 us -> 32.1 us  [on_device(): pl.pallas_call(kernel, out_shape=pltpu.VMEM((4, height, own), f32), in_sp...]
where the time goes in v3:
time: 33 us; the launch traced here: 32.9 us
  Pallas kernels  32.1 us (97%)
  local copies, waits for them, and re-layouts  0.71 us (2%)
    pallas_call x1, Pallas kernels, on_device(): pl.pallas_call(kernel, out_shape=pltpu.VMEM((4, height, own), f32), in_sp...  32.1 us
    unnamed x1, local copies, waits for them, and re-layouts  0.71 us

profile of v3, /device:TPU:1, one launch (start us, length us, event | category | flops | bytes accessed | tf_op | source)
XLA Modules:
  0.0 32.9 jit_solution(7203084846611815720)
XLA Ops:
  0.0 32.1 %render.1 = f32[4,64,256]{2,1,0:T(8,128)S(1)} custom-call(f32[8]{0:T(128)} %transfer.1, f32[48,64,2048]{2,1,0:T(8,128)} %volume.1), custom_call_target="tpu_custom_call" | custom-call | tf_op jit(solution)/shard_map/render/pallas_call | solution.py:421
  32.2 0.7 %copy.4 = f32[4,64,256]{2,1,0:T(8,128)} copy(f32[4,64,256]{2,1,0:T(8,128)S(1)} %render.1) | data formatting | bytes 524288

commit v4 on v3

--- a/solution.py
+++ b/solution.py
@@ -58,10 +58,8 @@
         )
 
     lead = 2 - 2 * core
-    order = [lead, lead + 1, lead + 15, lead + 2]
+    order = [lead + 15, lead, lead + 1, lead + 2]
     second = [3 * core, 15 + 5 * core]
-    for position in order + second:
-        load(position).start()
 
     def partners(act):
         for offset in (2, 4, 6):
@@ -80,6 +78,8 @@
         signal() if there is True else pl.when(there)(signal)
 
     partners(greet)
+    for position in order + second + list(range(11, 15)):
+        load(position).start()
 
     @pl.loop(0, slices)
     def _(z):
@@ -281,8 +281,6 @@
         def _():
             for position in order:
                 load(position).wait()
-            for position in range(11, 15):
-                load(position).start()
 
         @pl.when(step == 1)
         def _():

time: 33 us -> 32.9 us (level)
  no operation moved by 1% of the time
where the time goes in v4:
time: 32.9 us; the launch traced here: 32.8 us
  Pallas kernels  32.1 us (98%)
  local copies, waits for them, and re-layouts  0.71 us (2%)
    pallas_call x1, Pallas kernels, on_device(): pl.pallas_call(kernel, out_shape=pltpu.VMEM((4, height, own), f32), in_sp...  32.1 us
    unnamed x1, local copies, waits for them, and re-layouts  0.71 us

profile of v4, /device:TPU:1, one launch (start us, length us, event | category | flops | bytes accessed | tf_op | source)
XLA Modules:
  0.0 32.8 jit_solution(4354857336504832842)
XLA Ops:
  0.0 32.1 %render.1 = f32[4,64,256]{2,1,0:T(8,128)S(1)} custom-call(f32[8]{0:T(128)} %transfer.1, f32[48,64,2048]{2,1,0:T(8,128)} %volume.1), custom_call_target="tpu_custom_call" | custom-call | tf_op jit(solution)/shard_map/render/pallas_call | solution.py:419
  32.1 0.7 %copy.4 = f32[4,64,256]{2,1,0:T(8,128)} copy(f32[4,64,256]{2,1,0:T(8,128)S(1)} %render.1) | data formatting | bytes 524288

commit v5 on v4

--- a/solution.py
+++ b/solution.py
@@ -301,24 +301,25 @@
 
     @pl.loop(0, EARLY)
     def _(step):
+        @pl.when(step == 1)
+        def _():
+            pl.semaphore_wait(barrier, count)
+            send_halos((0, 1), 0)
+
         wait_loads(step)
 
         @pl.when(step == 1)
         def _():
-            pl.semaphore_wait(barrier, count)
-            send_halos((0, 1, 2, 3), 0)
-            send_halos((0, 1), 1)
+            send_halos((2, 3), 0)
 
         @pl.when(step == 2)
         def _():
-            send_halos((2, 3), 1)
-            send_halos((0, 1), 2)
-            send_halos((0, 1), 3)
+            send_halos((0, 1, 2, 3), 1)
 
         @pl.when(step == 4)
         def _():
-            send_halos((2, 3), 2)
-            send_halos((2, 3), 3)
+            send_halos((0, 1, 2, 3), 2)
+            send_halos((0, 1, 2, 3), 3)
 
         block = block_of(depth, step)
         march(2 * block, ROWS, step, False)

time: 32.9 us -> 32.9 us (level)
  no operation moved by 1% of the time
where the time goes in v5:
time: 32.9 us; the launch traced here: 32.8 us
  Pallas kernels  32.1 us (98%)
  local copies, waits for them, and re-layouts  0.71 us (2%)
    pallas_call x1, Pallas kernels, on_device(): pl.pallas_call(kernel, out_shape=pltpu.VMEM((4, height, own), f32), in_sp...  32.1 us
    unnamed x1, local copies, waits for them, and re-layouts  0.71 us

profile of v5, /device:TPU:1, one launch (start us, length us, event | category | flops | bytes accessed | tf_op | source)
XLA Modules:
  0.0 32.8 jit_solution(18059529662065852710)
XLA Ops:
  0.0 32.1 %render.1 = f32[4,64,256]{2,1,0:T(8,128)S(1)} custom-call(f32[8]{0:T(128)} %transfer.1, f32[48,64,2048]{2,1,0:T(8,128)} %volume.1), custom_call_target="tpu_custom_call" | custom-call | tf_op jit(solution)/shard_map/render/pallas_call | solution.py:420
  32.1 0.7 %copy.4 = f32[4,64,256]{2,1,0:T(8,128)} copy(f32[4,64,256]{2,1,0:T(8,128)S(1)} %render.1) | data formatting | bytes 524288
